TPU v7x, 512 devices: a whole 4x4x16 slice. The times are simulated.
512 devices in a mesh: wide: 64 (over x, z_lo, core), node: 8 (over z_hi, y).
Axes of the slice: x: 4, y: 4, z: 16 (z_hi: 2, z_lo: 8; z = z_hi * 8 + z_lo), core: 2. Of those that a mesh axis runs over, the one named last changes fastest.
Arguments:
- hidden: bfloat16 [8192, 24576], P('node', 'wide'), may hold values from -6 to 6
- cotangent: bfloat16 [8192, 4096], P(('node', 'wide')), may hold values from -6 to 6
- weight_codes: bfloat16 [4096, 24576], P('node', 'wide'), may hold values from -0.0390625 to 0.0390625
- block_scales: bfloat16 [32, 24576], P('node', 'wide'), may hold values from 0.25 to 4
Outputs:
- hidden_grad: bfloat16 [8192, 24576], P('node', 'wide')
- weight_grad: bfloat16 [4096, 24576], P('node', 'wide')
All inputs are finite; a program needn't handle non-finite values.
Results may differ from a plain program's by a relative error of at most 0.015.
Values may be sent and summed in bfloat16 or wider, within the bound.
A program may use at most 64 MiB of HBM per device.

v0:
```python
import jax
import jax.numpy as jnp
from jax import lax
from jax.sharding import PartitionSpec as P


def apply_scales(codes, scales):
    blocks = scales.shape[0]
    shaped = codes.astype(jnp.float32).reshape(blocks, codes.shape[0] // blocks, codes.shape[1])
    return (
        (shaped * scales.astype(jnp.float32)[:, None, :]).reshape(codes.shape).astype(jnp.bfloat16)
    )


def band_weight(weight_codes, block_scales):
    codes, scales = (
        lax.all_gather(weight_codes, "node", axis=0, tiled=True),
        lax.all_gather(block_scales, "node", axis=0, tiled=True),
    )
    return apply_scales(codes, scales)


def body(hidden, cotangent, weight_codes, block_scales):
    grad_scale = float(hidden.shape[0] * lax.axis_size("node")) ** (-0.5)
    contract_rows = (((0,), (0,)), ((), ()))
    gathered = lax.all_gather(cotangent, "wide", axis=0, tiled=True)
    full_weight = band_weight(weight_codes, block_scales)
    hidden_grad = jnp.dot(gathered, full_weight, preferred_element_type=jnp.float32)
    weight_grad = lax.psum_scatter(
        (
            grad_scale
            * lax.dot_general(gathered, hidden, contract_rows, preferred_element_type=jnp.float32)
        ).astype(jnp.bfloat16),
        "node",
        scatter_dimension=0,
        tiled=True,
    )
    return (hidden_grad.astype(jnp.bfloat16), weight_grad)


def solution(mesh):
    return jax.shard_map(
        body,
        mesh=mesh,
        in_specs=(
            P("node", "wide"),
            P(("node", "wide"), None),
            P("node", "wide"),
            P("node", "wide"),
        ),
        out_specs=(P("node", "wide"), P("node", "wide")),
        check_vma=False,
    )
```

profile of v0, /device:TPU:6, one launch (start us, length us, event | category | flops | bytes accessed | tf_op | source)
XLA Modules:
  0.0 472.6 jit_solution(17659494498807257031)
XLA Ops:
  7.2 0.0 copy-start
  7.2 0.0 all-gather.6.cloned.1.call-start
  7.2 0.7 all-gather.6.cloned.1.call-update
  7.9 0.0 all-gather.4.cloned.1.call-start
  8.0 0.7 all-gather.4.cloned.1.call-update
  8.7 0.0 copy-start.1
  8.7 0.0 reduce-scatter.2.cloned.1.call-start
  8.7 131.7 %all-gather.6.cloned.1.call-done = bf16[1024,4096]{1,0:T(8,128)(2,1)} async-done(((bf16[16,4096]{1,0:T(8,128)(2,1)}), bf16[1024,4096]{1,0:T(8,128)(2,1)}) %all-gather.6.cloned.1.call-update) | async-done | bytes 8388624 | tf_op jit(solution)/shard_map/all_gather | solution.py:26
  140.4 0.0 copy-done
  140.4 9.6 %multiply_convert_fusion = bf16[4096,384]{1,0:T(8,128)(2,1)} fusion(bf16[1024,4096]{1,0:T(8,128)(2,1)} %all-gather.6.cloned.1.call-done, bf16[1024,384]{1,0:T(8,128)(2,1)S(1)} %copy-done), kind=kOutput, calls=%fused_computation.2 | convolution fusion | flops 3224371200 | bytes 12320768 | tf_op jit(solution)/shard_map/dot_general | solution.py:32
  150.0 0.0 reduce-scatter.2.cloned.1.call-update
  150.0 0.0 copy-done.1
  150.0 77.7 %all-gather = bf16[8,4,384]{2,1,0:T(4,128)(2,1)S(1)} all-gather(bf16[1,4,384]{2,1,0:T(4,128)(2,1)S(1)} %bitcast.11), channel_id=1, replica_groups=mesh['wide'=64,'node'=8] {'node'}, dimensions={0}, use_global_device_ids=true | all-gather | bytes 27648 | tf_op jit(solution)/shard_map/all_gather | solution.py:18
  227.7 55.3 %all-gather.4.cloned.1.call-done = bf16[4096,384]{1,0:T(8,128)(2,1)} async-done(((bf16[512,384]{1,0:T(8,128)(2,1)}), bf16[4096,384]{1,0:T(8,128)(2,1)}) %all-gather.4.cloned.1.call-update) | async-done | bytes 3145744 | tf_op jit(solution)/shard_map/all_gather | solution.py:17
  283.0 2.5 fusion
  285.5 6.0 %fusion.1 = bf16[1024,384]{0,1:T(8,128)(2,1)S(1)} fusion(bf16[4096,384]{1,0:T(8,128)(2,1)S(1)} %fusion, bf16[1024,4096]{1,0:T(8,128)(2,1)} %all-gather.6.cloned.1.call-done), kind=kOutput, calls=%fused_computation.4 | convolution fusion | flops 3221618688 | bytes 12320768 | tf_op jit(solution)/shard_map/dot_general | solution.py:28
  291.5 1.2 copy.7
  292.7 173.4 %reduce-scatter.2.cloned.1.call-done = bf16[512,384]{1,0:T(8,128)(2,1)} async-done(((bf16[4096,384]{1,0:T(8,128)(2,1)}), bf16[512,384]{1,0:T(8,128)(2,1)}) %reduce-scatter.2.cloned.1.call-update) | async-done | bytes 393232 | tf_op jit(solution)/shard_map/reduce_scatter | solution.py:29
  (1 shorter events, 0.0 us)
Async XLA Ops:
  7.2 133.3 %copy-start = (bf16[1024,384]{1,0:T(8,128)(2,1)S(1)}, bf16[1024,384]{1,0:T(8,128)(2,1)}, u32[]{:S(2)}) copy-start(bf16[1024,384]{1,0:T(8,128)(2,1)} %param.4) | copy-start | bytes 2359300
  7.2 133.2 %all-gather.6.cloned.1.call-start = ((), (), s32[]{:S(2)}) async-start(), calls=%async_computation.2 | async-start | bytes 8519680 | tf_op jit(solution)/shard_map/all_gather | solution.py:26
  7.9 275.1 %all-gather.4.cloned.1.call-start = ((), (), s32[]{:S(2)}) async-start(), calls=%async_computation.1 | async-start | bytes 3538944 | tf_op jit(solution)/shard_map/all_gather | solution.py:17
  8.7 141.3 %copy-start.1 = (bf16[4,384]{1,0:T(4,128)(2,1)S(1)}, bf16[4,384]{1,0:T(4,128)(2,1)}, u32[]{:S(2)}) copy-start(bf16[4,384]{1,0:T(4,128)(2,1)} %param.7) | copy-start | bytes 9220
  8.7 457.4 %reduce-scatter.2.cloned.1.call-start = ((), (), s32[]{:S(2)}) async-start(), calls=%async_computation.3 | async-start | bytes 3538944 | tf_op jit(solution)/shard_map/reduce_scatter | solution.py:29
Sparse Core Ops, SparseCore 0:
  10.2 130.2 all-gather.5
  143.6 139.3 all-gather.3
  288.4 177.6 reduce-scatter.1
where the time goes:
time: 473 us
  waiting for transfers between devices  362 us (77%)
  blocking collectives  77.7 us (16%)
  matrix products  15.6 us (3%)
  between operations  13.8 us (3%)
    reduce_scatter x1, waiting for transfers between devices, body(): lax.psum_scatter((grad_scale * lax.dot_general(gathered, hidden, contract...  173 us
    all_gather x1, waiting for transfers between devices, body(): gathered = lax.all_gather(cotangent, 'wide', axis=0, tiled=True)  132 us
    all_gather x1, blocking collectives, band_weight(): lax.all_gather(block_scales, 'node', axis=0, tiled=True)  77.7 us
    all_gather x1, waiting for transfers between devices, band_weight(): lax.all_gather(weight_codes, 'node', axis=0, tiled=True)  55.3 us
    dot_general x1, matrix products, body(): lax.dot_general(gathered, hidden, contract_rows, preferred_element_type=j...  9.55 us
  transfers between devices with their start and end apart: 3, of which 3 were waited for; matrix products, arithmetic and copies ran while one was open for 4% of the time, Pallas kernels for 0%

commit v1 on v0

v1 whole, which is shorter than its diff:
```python
import functools

import jax
import jax.numpy as jnp
from jax import lax
from jax.experimental import pallas as pl
from jax.experimental.pallas import tpu as pltpu
from jax.sharding import PartitionSpec as P

MESH = pl.DeviceIdType.MESH
NX, NY, NZ = 4, 4, 8
D, FB, TOK, ROWS, QB = 4096, 384, 1024, 16, 128
OWN = D // 8
HALF = D // 2
FZ = 2
F32, BF16 = jnp.float32, jnp.bfloat16


def kernel(
    hid_hbm, cot_hbm, codes_hbm, scales_ref,
    hgrad_ref, wgrad_ref,
    cot, hid, hid_t, codes, weight, part, ywhole, yhalf, zsum, zgot, near_sum, hacc,
    local_sem, z_s, z_r, x_s, x_r, xh_s, xh_r, c_s, c_r,
    wy_s, wy_r, wh_s, wh_r, wz_s, wz_r, gy_s, gy_r, gh_s, gh_r, gz_s, gz_r,
):
    wide, node = lax.axis_index("wide"), lax.axis_index("node")
    x, zl, core = wide // (2 * NZ), (wide // 2) % NZ, wide % 2
    zh, y = node // NY, node % NY

    def at(dx=0, dy=0, dz=0):
        z = (zh * NZ + zl + dz + 2 * NZ) % (2 * NZ)
        return (
            ((x + dx + NX) % NX) * 2 * NZ + (z % NZ) * 2 + core,
            (z // NZ) * NY + (y + dy + NY) % NY,
        )

    sibling = (wide + 1 - 2 * core, node)
    right_of = {"x": at(dx=1), "y": at(dy=1), "z": at(dz=1)}
    left_of = {"x": at(dx=-1), "y": at(dy=-1), "z": at(dz=-1)}
    across = at(dz=NZ)
    sent = []

    def remote(src, dst, s, r, to):
        return pltpu.make_async_remote_copy(
            src_ref=src, dst_ref=dst, send_sem=s, recv_sem=r, device_id=to, device_id_type=MESH
        )

    def send(src, dst, s, r, to):
        copy = remote(src, dst, s, r, to)
        copy.start()
        sent.append((None, copy))

    def landed(dst, r):
        remote(dst, dst, r, r, sibling).wait_recv()

    barrier = pltpu.get_barrier_semaphore()
    peers = [*right_of.values(), *left_of.values(), sibling, across]
    for peer in peers:
        pl.semaphore_signal(barrier, inc=1, device_id=peer, device_id_type=MESH)
    loads = [
        pltpu.make_async_copy(cot_hbm, cot.at[wide], local_sem.at[0]),
        pltpu.make_async_copy(codes_hbm, codes, local_sem.at[1]),
        pltpu.make_async_copy(hid_hbm, hid, local_sem.at[2]),
    ]
    for load in loads:
        load.start()
    loads[0].wait()
    pl.semaphore_wait(barrier, len(peers))

    def block(dx, z):
        return ((x + dx + NX) % NX) * 2 * NZ + z * 2 + core

    fz = D // FZ

    def spread(z):
        b = block(0, z)
        for d, to in ((0, right_of["x"]), (1, left_of["x"])):
            remote(cot.at[b], cot.at[b], x_s.at[d, z], x_r.at[d, z], to).start()
        remote(cot.at[b], cot.at[b], c_s.at[0, z], c_r.at[0, z], sibling).start()

    def pass_on(z, f, d):
        b = block(0, z)
        piece = cot.at[b, :, pl.ds(f * fz, fz)]
        to = (right_of["z"], left_of["z"])[d]
        return remote(piece, piece, z_s.at[d, z, f], z_r.at[z, f], to)

    for f in range(FZ):
        for d, edge in ((0, zl < NZ - 1), (1, zl > 0)):

            @pl.when(edge)
            def _():
                pass_on(zl, f, d).start()

    spread(zl)

    loads[1].wait()
    for q in range(OWN // QB):
        rows = pl.ds(q * QB, QB)
        weight[node, rows, :] = (
            codes[rows, :].astype(F32) * scales_ref[pl.ds(q, 1), :].astype(F32)
        ).astype(BF16)

    def weight_y(k, n):
        for d, to in ((0, right_of["y"]), (1, left_of["y"])):
            send(weight.at[n], weight.at[n], wy_s.at[k, d], wy_r.at[k, d], to)

    def near(dy):
        return zh * NY + (y + dy + NY) % NY

    def far(dy):
        return (1 - zh) * NY + (y + dy + NY) % NY

    def of(k, dy):
        return (near, far)[k](dy)

    weight_y(0, node)

    for s in range(1, NZ):
        for d in range(2):
            z = zl - s if d == 0 else zl + s
            there = z >= 0 if d == 0 else z < NZ

            @pl.when(there)
            def _():
                for f in range(FZ):
                    piece = cot.at[block(0, z), :, pl.ds(f * fz, fz)]
                    landed(piece, z_r.at[z, f])

                    @pl.when(zl < NZ - 1 if d == 0 else zl > 0)
                    def _():
                        pass_on(z, f, d).start()

                spread(z)

    loads[2].wait()
    hid_t[...] = hid[...].T

    def weight_forward(k):
        for d, to in ((0, right_of["y"]), (1, left_of["y"])):
            n = of(k, -1 if d == 0 else 1)
            landed(weight.at[n], wy_r.at[k, d])
            half = weight.at[n, pl.ds(d * (OWN // 2), OWN // 2), :]
            send(half, half, wh_s.at[k, d], wh_r.at[k, d], to)

    weight_forward(0)

    def slots():
        for s in range(NZ):
            for d in range(2 if s else 1):
                z = zl - s if d == 0 else zl + s
                yield s, z, (z >= 0 if d == 0 else z < NZ)

    for s, z, there in slots():
        @pl.when(there)
        def _():
            for d, to in ((0, right_of["x"]), (1, left_of["x"])):
                b = block(-1 if d == 0 else 1, z)
                landed(cot.at[b], x_r.at[d, z])
                half = cot.at[b, :, pl.ds(d * HALF, HALF)]
                remote(half, half, xh_s.at[d, z], xh_r.at[d, z], to).start()
                remote(cot.at[b], cot.at[b], c_s.at[1 + d, z], c_r.at[1 + d, z], sibling).start()

        if s == 3 :
            pass
    send(weight.at[node], weight.at[node], wz_s.at[0], wz_r.at[0], across)
    for s, z, there in slots():
        @pl.when(there)
        def _():
            for d in range(2):
                half = cot.at[block(2, z), :, pl.ds(d * HALF, HALF)]
                landed(half, xh_r.at[d, z])
                remote(half, half, c_s.at[3 + d, z], c_r.at[3 + d, z], sibling).start()

    def other(dx, z):
        return block(dx, z) + 1 - 2 * core

    for z in range(NZ):
        landed(cot.at[other(0, z)], c_r.at[0, z])
        landed(cot.at[other(-1, z)], c_r.at[1, z])
        landed(cot.at[other(1, z)], c_r.at[2, z])
        for d in range(2):
            landed(cot.at[other(2, z), :, pl.ds(d * HALF, HALF)], c_r.at[3 + d, z])

    def term(n):
        @pl.loop(0, OWN // 256)
        def _(i):
            columns = pl.ds(pl.multiple_of(n * OWN + i * 256, 256), 256)
            rows = cot[:, :, columns].reshape(TOK, 256)
            part[n, :, pl.ds(pl.multiple_of(i * 256, 256), 256)] = jnp.dot(
                hid_t[...], rows, preferred_element_type=F32
            ).astype(BF16)

    hb = FB // 2

    def start_halves(k):
        n = of(k, 2)
        term(n)
        for d, to in ((0, right_of["y"]), (1, left_of["y"])):
            send(
                part.at[n, pl.ds(d * hb, hb), :], yhalf.at[k, d], gh_s.at[k, d], gh_r.at[k, d], to
            )

    def send_neighbours(k):
        for d, to in ((0, right_of["y"]), (1, left_of["y"])):
            n = of(k, 1 if d == 0 else -1)
            landed(yhalf.at[k, d], gh_r.at[k, d])
            rows = pl.ds(d * hb, hb)
            part[n, rows, :] = (
                part[n, rows, :].astype(F32) + yhalf[k, d].astype(F32)
            ).astype(BF16)
            send(part.at[n], ywhole.at[k, d], gy_s.at[k, d], gy_r.at[k, d], to)

    def summed(k):
        for d in range(2):
            landed(ywhole.at[k, d], gy_r.at[k, d])
        return (
            part[of(k, 0)].astype(F32) + ywhole[k, 0].astype(F32) + ywhole[k, 1].astype(F32)
        )

    def hidden_part(k, last):
        @pl.loop(0, TOK // 256)
        def _(i):
            first = pl.multiple_of(i * 256, 256)
            half = (zh if k == 0 else 1 - zh) * HALF
            rows = cot[pl.ds(pl.multiple_of(i * 16, 16), 16), :, pl.ds(pl.multiple_of(half, HALF), HALF)]
            group = (zh if k == 0 else 1 - zh) * NY
            product = jnp.dot(
                rows.reshape(256, HALF),
                weight[pl.ds(group, NY)].reshape(HALF, FB),
                preferred_element_type=F32,
            )
            if last:
                hgrad_ref[pl.ds(first, 256), :] = (hacc[pl.ds(first, 256), :] + product).astype(BF16)
            else:
                hacc[pl.ds(first, 256), :] = product

    def weight_halves(k):
        for d in range(2):
            landed(
                weight.at[of(k, 2), pl.ds(d * (OWN // 2), OWN // 2), :], wh_r.at[k, d]
            )

    start_halves(1)
    term(far(1))
    term(far(-1))
    send_neighbours(1)
    term(far(0))
    start_halves(0)
    term(near(1))
    term(near(-1))
    term(near(0))
    zsum[...] = summed(1).astype(BF16)
    send(zsum, zgot, gz_s.at[0], gz_r.at[0], across)
    send_neighbours(0)
    weight_halves(0)
    hidden_part(0, False)
    near_sum[...] = summed(0)
    landed(weight.at[far(0)], wz_r.at[0])
    weight_y(1, far(0))
    weight_forward(1)
    weight_halves(1)
    hidden_part(1, True)
    landed(zgot, gz_r.at[0])
    total = (near_sum[...] + zgot[...].astype(F32)) * float(TOK * 8) ** -0.5
    wgrad_ref[...] = total.T.astype(BF16)

    for _, copy in sent:
        copy.wait_send()
    for z in range(NZ):
        for d in range(2):
            whole = cot.at[block(0, z)]
            remote(whole, whole, x_s.at[d, z], x_r.at[d, z], sibling).wait_send()
            half = cot.at[block(0, z), :, pl.ds(d * HALF, HALF)]
            remote(half, half, xh_s.at[d, z], xh_r.at[d, z], sibling).wait_send()
            remote(half, half, c_s.at[3 + d, z], c_r.at[3 + d, z], sibling).wait_send()
        for j in range(3):
            remote(whole, whole, c_s.at[j, z], c_r.at[j, z], sibling).wait_send()
        for d in range(2):
            passed = jnp.logical_and(z <= zl, zl < NZ - 1) if d == 0 else jnp.logical_and(z >= zl, zl > 0)

            @pl.when(passed)
            def _():
                for f in range(FZ):
                    pass_on(z, f, d).wait_send()


def body(hidden, cotangent, weight_codes, block_scales):
    dma = pltpu.SemaphoreType.DMA
    hbm = pl.BlockSpec(memory_space=pl.ANY)
    vmem = pl.BlockSpec(memory_space=pltpu.VMEM)
    return pl.pallas_call(
        kernel,
        out_shape=(
            jax.ShapeDtypeStruct((TOK, FB), BF16),
            jax.ShapeDtypeStruct((OWN, FB), BF16),
        ),
        in_specs=[hbm, hbm, hbm, vmem],
        out_specs=(vmem, vmem),
        scratch_shapes=[
            pltpu.VMEM((2 * NX * NZ, ROWS, D), BF16),
            pltpu.VMEM((TOK, FB), BF16),
            pltpu.VMEM((FB, TOK), BF16),
            pltpu.VMEM((OWN, FB), BF16),
            pltpu.VMEM((8, OWN, FB), BF16),
            pltpu.VMEM((8, FB, OWN), BF16),
            pltpu.VMEM((2, 2, FB, OWN), BF16),
            pltpu.VMEM((2, 2, FB // 2, OWN), BF16),
            pltpu.VMEM((FB, OWN), BF16),
            pltpu.VMEM((FB, OWN), BF16),
            pltpu.VMEM((FB, OWN), F32),
            pltpu.VMEM((TOK, FB), F32),
            dma((3,)),
            dma((2, NZ, FZ)), dma((NZ, FZ)),
            dma((2, NZ)), dma((2, NZ)), dma((2, NZ)), dma((2, NZ)),
            dma((5, NZ)), dma((5, NZ)),
            dma((2, 2)), dma((2, 2)), dma((2, 2)), dma((2, 2)),
            dma((1,)), dma((1,)),
            dma((2, 2)), dma((2, 2)), dma((2, 2)), dma((2, 2)),
            dma((1,)), dma((1,)),
        ],
        compiler_params=pltpu.CompilerParams(
            collective_id=0, has_side_effects=True, vmem_limit_bytes=56 << 20
        ),
        cost_estimate=pl.CostEstimate(
            flops=4 * TOK * D * FB, bytes_accessed=4 << 20, transcendentals=0
        ),
    )(hidden, cotangent, weight_codes, block_scales)


def solution(mesh):
    return jax.shard_map(
        body,
        mesh=mesh,
        in_specs=(
            P("node", "wide"),
            P(("node", "wide"), None),
            P("node", "wide"),
            P("node", "wide"),
        ),
        out_specs=(P("node", "wide"), P("node", "wide")),
        check_vma=False,
    )
```

time: 473 us -> 138 us (0.29)
  waiting for transfers between devices: 362 us -> 0 us
  Pallas kernels: 0 us -> 134 us
  blocking collectives: 77.7 us -> 0 us
  matrix products: 15.6 us -> 0 us
  between operations: 13.8 us -> 0.65 us
    all_gather x2 -> x0, waiting for transfers between devices: 187 us -> none  [the longest x1 132 us: body(): gathered = lax.all_gather(cotangent, 'wide', axis=0, tiled=True)]
    reduce_scatter x1 -> x0, waiting for transfers between devices: 173 us -> none  [body(): lax.psum_scatter((grad_scale * lax.dot_general(gathered, hidden, contract...]
    pallas_call x0 -> x1, Pallas kernels: none -> 134 us  [body(): pl.pallas_call(kernel, out_shape=(jax.ShapeDtypeStruct((TOK, FB), BF16),...]
    all_gather x1 -> x0, blocking collectives: 77.7 us -> none  [band_weight(): lax.all_gather(block_scales, 'node', axis=0, tiled=True)]
    dot_general x2 -> x0, matrix products: 15.6 us -> none  [the longest x1 9.55 us: body(): lax.dot_general(gathered, hidden, contract_rows, preferred_element_type=j...]
  transfers between devices with their start and end apart: 3 -> 0, of which waited for: 3 -> 0; matrix products, arithmetic and copies ran while one was open for 4% -> 0% of each run, Pallas kernels for 0% -> 0%
where the time goes in v1:
time: 138 us; the launch traced here: 137 us
  Pallas kernels  134 us (97%)
  local copies, waits for them, and re-layouts  2.89 us (2%)
    pallas_call x1, Pallas kernels, body(): pl.pallas_call(kernel, out_shape=(jax.ShapeDtypeStruct((TOK, FB), BF16),...  134 us
    unnamed x4, local copies, waits for them, and re-layouts  2.89 us

profile of v1, /device:TPU:6, one launch (start us, length us, event | category | flops | bytes accessed | tf_op | source)
XLA Modules:
  0.0 137.4 jit_solution(12797515517889563445)
XLA Ops:
  0.6 133.8 %shard_map.59 = (bf16[1024,384]{1,0:T(8,128)(2,1)}, bf16[512,384]{1,0:T(8,128)(2,1)}) custom-call(bf16[1024,384]{1,0:T(8,128)(2,1)} %hid_hbm.1, bf16[16,4096]{1,0:T(8,128)(2,1)} %cot_hbm.1, bf16[512,384]{1,0:T(8,128)(2,1)} %codes_hbm.1, bf16[4,384]{1,0:T(4,128)(2,1)} %scales_ref.1), custom_call_target="tpu_custom_call" | custom-call | flops 6442450944 | bytes 4194304 | tf_op jit(solution)/shard_map/pallas_call | solution.py:291
  134.5 0.0 copy-start
  134.5 2.1 %copy.8 = bf16[1024,384]{1,0:T(8,128)(2,1)} copy(bf16[1024,384]{1,0:T(8,128)(2,1)} %get-tuple-element.4) | data formatting | bytes 1572864
  136.6 0.0 copy-done
  136.6 0.7 copy.9
Async XLA Ops:
  134.5 2.2 %copy-start = (bf16[512,384]{1,0:T(8,128)(2,1)S(1)}, bf16[512,384]{1,0:T(8,128)(2,1)}, u32[]{:S(2)}) copy-start(bf16[512,384]{1,0:T(8,128)(2,1)} %get-tuple-element.5) | copy-start | bytes 1179652

commit v2 on v0

v2 whole, which is shorter than its diff:
```python
import functools

import jax
import jax.numpy as jnp
from jax import lax
from jax.experimental import pallas as pl
from jax.experimental.pallas import tpu as pltpu
from jax.sharding import PartitionSpec as P

MESH = pl.DeviceIdType.MESH
NX, NY, NZ = 4, 4, 8
D, FB, TOK, ROWS, QB = 4096, 384, 1024, 16, 128
OWN = D // 8
HALF = D // 2
FZ = 2
CW = 4
CG = 3
F32, BF16 = jnp.float32, jnp.bfloat16


def schedule():
    return [('own',), ('weights',), ('turn',), ('z', 1, 0), ('z', 1, 1), ('xf', 0), ('z', 2, 0), ('z', 2, 1), ('z', 3, 0), ('z', 3, 1), ('xf', 1), ('near_weights',), ('z', 4, 0), ('xh', 0), ('z', 4, 1), ('w', 0, 0), ('w', 0, 1), ('w', 0, 2), ('w', 0, 3), ('z', 5, 0), ('z', 5, 1), ('xf', 2), ('near_halves',), ('w', 1, 0), ('w', 1, 1), ('z', 6, 0), ('z', 6, 1), ('w', 1, 2), ('xf', 3), ('w', 1, 3), ('z', 7, 0), ('z', 7, 1), ('xh', 1), ('w', 2, 0), ('w', 2, 1), ('w', 2, 2), ('xf', 4), ('w', 2, 3), ('xh', 2), ('xf', 5), ('w', 3, 0), ('w', 3, 1), ('w', 3, 2), ('xf', 6), ('xh', 3), ('w', 3, 3), ('xf', 7), ('xh', 6), ('w', 4, 0), ('xh', 7), ('xh', 4), ('xh', 5), ('w', 4, 1), ('w', 4, 2), ('w', 4, 3), ('w', 5, 0), ('cores',), ('term', 1, 2), ('w', 5, 1), ('gh', 1, 0), ('gh', 1, 1), ('gh', 1, 2), ('term', 1, 1), ('term', 1, -1), ('w', 5, 2), ('w', 5, 3), ('term', 1, 0), ('term', 0, 2), ('gn', 1, 0), ('gh', 0, 0), ('gh', 0, 1), ('gh', 0, 2), ('term', 0, 1), ('w', 6, 0), ('gn', 1, 1), ('term', 0, -1), ('w', 6, 1), ('term', 0, 0), ('gn', 1, 2), ('hid', 0, 0), ('w', 6, 2), ('hid', 0, 1), ('hid', 0, 2), ('w', 6, 3), ('gs', 0), ('hid', 0, 3), ('w', 7, 0), ('gn', 0, 0), ('w', 7, 1), ('gn', 0, 1), ('w', 7, 2), ('w', 7, 3), ('gn', 0, 2), ('g', 1, 0), ('gs', 1), ('far_weights',), ('gs', 2), ('g', 2, 0), ('g', 1, 1), ('ns', 0), ('g', 1, 2), ('g', 3, 0), ('ns', 1), ('g', 2, 1), ('g', 2, 2), ('ns', 2), ('g', 4, 0), ('g', 3, 1), ('g', 3, 2), ('g', 5, 0), ('g', 4, 1), ('g', 4, 2), ('far_forward',), ('g', 6, 0), ('g', 5, 1), ('g', 5, 2), ('g', 7, 0), ('far_halves',), ('hid', 1, 0), ('hid', 1, 1), ('g', 6, 1), ('hid', 1, 2), ('hid', 1, 3), ('g', 6, 2), ('left', 0), ('end', 0), ('g', 7, 1), ('g', 7, 2), ('end', 1), ('end', 2)]


def kernel(
    hid_hbm, cot_hbm, codes_hbm, scales_ref,
    hgrad_ref, wgrad_ref,
    cot, hid, hid_t, codes, weight, part, ywhole, yhalf, wrelay, grelay, near_sum, hacc,
    local_sem, z_s, z_r, x_s, x_r, xh_s, xh_r, c_s, c_r,
    wy_s, wy_r, wh_s, wh_r, wz_s, wz_r, gy_s, gy_r, gh_s, gh_r, gz_s, gz_r,
):
    wide, node = lax.axis_index("wide"), lax.axis_index("node")
    x, zl, core = wide // (2 * NZ), (wide // 2) % NZ, wide % 2
    zh, y = node // NY, node % NY

    def at(dx=0, dy=0, dz=0):
        z = (zh * NZ + zl + dz + 2 * NZ) % (2 * NZ)
        return (
            ((x + dx + NX) % NX) * 2 * NZ + (z % NZ) * 2 + core,
            (z // NZ) * NY + (y + dy + NY) % NY,
        )

    sibling = (wide + 1 - 2 * core, node)
    ways_x = (at(dx=1), at(dx=-1))
    ways_y = (at(dy=1), at(dy=-1))
    ways_z = (at(dz=1), at(dz=-1))
    def remote(src, dst, s, r, to):
        return pltpu.make_async_remote_copy(
            src_ref=src, dst_ref=dst, send_sem=s, recv_sem=r, device_id=to, device_id_type=MESH
        )

    def send(src, dst, s, r, to):
        remote(src, dst, s, r, to).start()

    def landed(dst, r):
        remote(dst, dst, r, r, sibling).wait_recv()

    def left(src, s):
        remote(src, src, s, s, sibling).wait_send()

    def block(dx, z):
        return ((x + dx + NX) % NX) * 2 * NZ + z * 2 + core

    def near(dy):
        return zh * NY + (y + dy + NY) % NY

    def far(dy):
        return (1 - zh) * NY + (y + dy + NY) % NY

    def of(k, dy):
        return (near, far)[k](dy)


    fz = D // FZ

    def pass_on(z, f, d):
        piece = cot.at[block(0, z), :, pl.ds(f * fz, fz)]
        return remote(piece, piece, z_s.at[d], z_r.at[z, f], ways_z[d])

    def spread(z):
        b = block(0, z)
        for d in range(2):
            remote(cot.at[b], cot.at[b], x_s.at[0], x_r.at[z], ways_x[d]).start()
        remote(cot.at[b], cot.at[b], c_s.at[0], c_r.at[0], sibling).start()

    def go_own():
        for f in range(FZ):
            for d, inside in ((0, zl < NZ - 1), (1, zl > 0)):

                @pl.when(inside)
                def _():
                    pass_on(zl, f, d).start()

        spread(zl)

    def sides(s):
        return [(0, zl - s, zl - s >= 0), (1, zl + s, zl + s < NZ)][: 2 if s else 1]

    def go_z(s, f):
        for d, z, there in sides(s):

            @pl.when(there)
            def _():
                landed(cot.at[block(0, z), :, pl.ds(f * fz, fz)], z_r.at[z, f])

                @pl.when(zl < NZ - 1 if d == 0 else zl > 0)
                def _():
                    pass_on(z, f, d).start()

                if f == FZ - 1:
                    spread(z)

    def half_of(dx, z, d):
        return cot.at[block(dx, z), :, pl.ds(d * HALF, HALF)]

    def go_xf(s):
        for _, z, there in sides(s):

            @pl.when(there)
            def _():
                landed(cot.at[pl.ds(0, 2)], x_r.at[z])
                for d, dx in ((0, -1), (1, 1)):
                    half = half_of(dx, z, d)
                    send(half, half, xh_s.at[0], xh_r.at[z], ways_x[d])
                for dx in (-1, 1):
                    b = block(dx, z)
                    send(cot.at[b], cot.at[b], c_s.at[0], c_r.at[0], sibling)

    def go_xh(s):
        for _, z, there in sides(s):

            @pl.when(there)
            def _():
                b = block(2, z)
                landed(cot.at[b], xh_r.at[z])
                send(cot.at[b], cot.at[b], c_s.at[0], c_r.at[0], sibling)

    def go_cores():
        landed(cot.at[pl.ds(0, NX * NZ)], c_r.at[0])


    def weight_y(k):
        n = of(k, 0)
        for d in range(2):
            send(weight.at[n], weight.at[n], wy_s.at[0], wy_r.at[k, d], ways_y[d])

    def weight_forward(k):
        for d in range(2):
            n = of(k, -1 if d == 0 else 1)
            landed(weight.at[n], wy_r.at[k, d])
            half = weight.at[n, pl.ds(d * (OWN // 2), OWN // 2), :]
            send(half, half, wh_s.at[0], wh_r.at[k], ways_y[d])

    def weight_halves(k):
        landed(weight.at[of(k, 2)], wh_r.at[k])

    def go_weights():
        loads[1].wait()
        for q in range(OWN // QB):
            rows = pl.ds(q * QB, QB)
            weight[node, rows, :] = (
                codes[rows, :].astype(F32) * scales_ref[pl.ds(q, 1), :].astype(F32)
            ).astype(BF16)
        weight_y(0)

    cw = OWN // 2 // CW

    def weight_piece(n, d, c):
        return weight.at[n, pl.ds(d * (OWN // 2) + c * cw, cw), :]

    def go_w(s, c):
        if s:
            landed(wrelay.at[s - 1, c], wz_r.at[s - 1, c])
        for d in range(2):
            src = weight_piece(node, d, c) if s == 0 else wrelay.at[s - 1, c, d]
            dst = wrelay.at[s, c, d]
            if s == NZ - 1:
                z = zh * NZ + zl + (1 if d == 0 else -1) + 2 * NZ
                dst = weight_piece((1 - (z // NZ) % 2) * NY + y, d, c)
            send(src, dst, wz_s.at[0], wz_r.at[s, c], ways_z[d])

    def go_far_weights():
        for c in range(CW):
            landed(wrelay.at[0, c], wz_r.at[NZ - 1, c])
        weight_y(1)


    def go_turn():
        loads[2].wait()
        hid_t[...] = hid[...].T

    def go_term(k, dy):
        n = of(k, dy)

        @pl.loop(0, 2)
        def _(i):
            columns = pl.ds(pl.multiple_of(n * OWN + i * (OWN // 2), OWN // 2), OWN // 2)
            rows = cot[:, :, columns].reshape(TOK, OWN // 2)
            part[n, i] = jnp.dot(hid_t[...], rows, preferred_element_type=F32).astype(BF16)

    cg = FB // CG

    def units(c):
        return pl.ds(c * cg, cg)

    def go_gh(k, c):
        for d in range(2):
            send(
                part.at[of(k, 2), d, units(c), :], yhalf.at[k, d, units(c), :],
                gh_s.at[0], gh_r.at[k, c], ways_y[d],
            )

    def go_gn(k, c):
        landed(yhalf.at[k, :, units(c), :], gh_r.at[k, c])
        for d in range(2):
            n = of(k, 1 if d == 0 else -1)
            part[n, d, units(c), :] = (
                part[n, d, units(c), :].astype(F32) + yhalf[k, d, units(c), :].astype(F32)
            ).astype(BF16)
            send(
                part.at[n, :, units(c), :], ywhole.at[k, d, :, units(c), :],
                gy_s.at[0], gy_r.at[k, c], ways_y[d],
            )

    def summed(k, c):
        landed(ywhole.at[k, :, :, units(c), :], gy_r.at[k, c])
        return (
            part[of(k, 0), :, units(c), :].astype(F32)
            + ywhole[k, 0, :, units(c), :].astype(F32)
            + ywhole[k, 1, :, units(c), :].astype(F32)
        )

    def go_gs(c):
        grelay[0, c] = summed(1, c).astype(BF16)
        go_g(0, c)

    def go_g(s, c):
        if s:
            landed(grelay.at[s, c], gz_r.at[s - 1, c])
        for d in range(2):
            send(
                grelay.at[s, c, d], grelay.at[s + 1, c, d], gz_s.at[0], gz_r.at[s, c], ways_z[d]
            )

    def go_ns(c):
        near_sum[:, units(c), :] = summed(0, c)

    def go_end(c):
        landed(grelay.at[NZ, c], gz_r.at[NZ - 1, c])
        for d in range(2):
            total = near_sum[d, units(c), :] + grelay[NZ, c, d].astype(F32)
            wgrad_ref[pl.ds(d * (OWN // 2), OWN // 2), units(c)] = (
                (total * float(TOK * 8) ** -0.5).T.astype(BF16)
            )


    def go_hid(k, i):
        rows = pl.ds(i * 256, 256)
        group = zh if k == 0 else 1 - zh
        features = pl.ds(pl.multiple_of(group * HALF, HALF), HALF)
        product = jnp.dot(
            cot[pl.ds(i * 16, 16), :, features].reshape(256, HALF),
            weight[pl.ds(group * NY, NY)].reshape(HALF, FB),
            preferred_element_type=F32,
        )
        if k == 0:
            hacc[rows, :] = product
        else:
            hgrad_ref[rows, :] = (hacc[rows, :] + product).astype(BF16)

    def go_left(k):
        if k:
            left(grelay.at[pl.ds(0, NZ)], gz_s.at[0])
            return
        left(cot.at[pl.ds(0, 2 * NZ)], x_s.at[0])
        left(cot.at[pl.ds(0, NZ)], xh_s.at[0])
        left(cot.at[pl.ds(0, NX * NZ)], c_s.at[0])
        for z in range(1, NZ):

            @pl.when(zl == z - 1)
            def _():
                left(cot.at[pl.ds(0, z)], z_s.at[0])

            @pl.when(zl == NZ - z)
            def _():
                left(cot.at[pl.ds(0, z)], z_s.at[1])

        left(weight.at[pl.ds(0, 4)], wy_s.at[0])
        left(weight.at[pl.ds(0, 2)], wh_s.at[0])
        left(weight, wz_s.at[0])
        left(part.at[pl.ds(0, 2)], gh_s.at[0])
        left(part.at[pl.ds(0, 4)], gy_s.at[0])

    barrier = pltpu.get_barrier_semaphore()
    peers = [*ways_x, *ways_y, *ways_z, sibling]
    for peer in peers:
        pl.semaphore_signal(barrier, inc=1, device_id=peer, device_id_type=MESH)
    loads = [
        pltpu.make_async_copy(cot_hbm, cot.at[wide], local_sem.at[0]),
        pltpu.make_async_copy(codes_hbm, codes, local_sem.at[1]),
        pltpu.make_async_copy(hid_hbm, hid, local_sem.at[2]),
    ]
    for load in loads:
        load.start()
    loads[0].wait()
    pl.semaphore_wait(barrier, len(peers))

    steps = {
        "own": go_own, "weights": go_weights, "z": go_z, "xf": go_xf, "xh": go_xh, "cores": go_cores,
        "near_weights": functools.partial(weight_forward, 0), "turn": go_turn, "w": go_w,
        "far_weights": go_far_weights, "far_forward": functools.partial(weight_forward, 1),
        "near_halves": functools.partial(weight_halves, 0),
        "far_halves": functools.partial(weight_halves, 1),
        "term": go_term, "gh": go_gh, "gn": go_gn, "gs": go_gs, "g": go_g, "ns": go_ns,
        "hid": go_hid, "end": go_end, "left": go_left,
    }
    for name, *where in schedule():
        steps[name](*where)

    go_left(1)


def body(hidden, cotangent, weight_codes, block_scales):
    dma = pltpu.SemaphoreType.DMA
    hbm = pl.BlockSpec(memory_space=pl.ANY)
    vmem = pl.BlockSpec(memory_space=pltpu.VMEM)
    return pl.pallas_call(
        kernel,
        out_shape=(
            jax.ShapeDtypeStruct((TOK, FB), BF16),
            jax.ShapeDtypeStruct((OWN, FB), BF16),
        ),
        in_specs=[hbm, hbm, hbm, vmem],
        out_specs=(vmem, vmem),
        scratch_shapes=[
            pltpu.VMEM((2 * NX * NZ, ROWS, D), BF16),
            pltpu.VMEM((TOK, FB), BF16),
            pltpu.VMEM((FB, TOK), BF16),
            pltpu.VMEM((OWN, FB), BF16),
            pltpu.VMEM((8, OWN, FB), BF16),
            pltpu.VMEM((8, 2, FB, OWN // 2), BF16),
            pltpu.VMEM((2, 2, 2, FB, OWN // 2), BF16),
            pltpu.VMEM((2, 2, FB, OWN // 2), BF16),
            pltpu.VMEM((NZ - 1, CW, 2, OWN // 2 // CW, FB), BF16),
            pltpu.VMEM((NZ + 1, CG, 2, FB // CG, OWN // 2), BF16),
            pltpu.VMEM((2, FB, OWN // 2), F32),
            pltpu.VMEM((TOK, FB), F32),
            dma((3,)),
            dma((2,)), dma((NZ, FZ)),
            dma((1,)), dma((NZ,)), dma((1,)), dma((NZ,)),
            dma((1,)), dma((1,)),
            dma((1,)), dma((2, 2)), dma((1,)), dma((2,)),
            dma((1,)), dma((NZ, CW)),
            dma((1,)), dma((2, CG)), dma((1,)), dma((2, CG)),
            dma((1,)), dma((NZ, CG)),
        ],
        compiler_params=pltpu.CompilerParams(
            collective_id=0, has_side_effects=True, vmem_limit_bytes=56 << 20
        ),
        cost_estimate=pl.CostEstimate(
            flops=4 * TOK * D * FB, bytes_accessed=4 << 20, transcendentals=0
        ),
    )(hidden, cotangent, weight_codes, block_scales)


def solution(mesh):
    return jax.shard_map(
        body,
        mesh=mesh,
        in_specs=(
            P("node", "wide"),
            P(("node", "wide"), None),
            P("node", "wide"),
            P("node", "wide"),
        ),
        out_specs=(P("node", "wide"), P("node", "wide")),
        check_vma=False,
    )
```

time: 473 us -> 119 us (0.25)
  waiting for transfers between devices: 362 us -> 0 us
  Pallas kernels: 0 us -> 115 us
  blocking collectives: 77.7 us -> 0 us
  matrix products: 15.6 us -> 0 us
  between operations: 13.8 us -> 0.65 us
    all_gather x2 -> x0, waiting for transfers between devices: 187 us -> none  [the longest x1 132 us: body(): gathered = lax.all_gather(cotangent, 'wide', axis=0, tiled=True)]
    reduce_scatter x1 -> x0, waiting for transfers between devices: 173 us -> none  [body(): lax.psum_scatter((grad_scale * lax.dot_general(gathered, hidden, contract...]
    pallas_call x0 -> x1, Pallas kernels: none -> 115 us  [body(): pl.pallas_call(kernel, out_shape=(jax.ShapeDtypeStruct((TOK, FB), BF16),...]
    all_gather x1 -> x0, blocking collectives: 77.7 us -> none  [band_weight(): lax.all_gather(block_scales, 'node', axis=0, tiled=True)]
    dot_general x2 -> x0, matrix products: 15.6 us -> none  [the longest x1 9.55 us: body(): lax.dot_general(gathered, hidden, contract_rows, preferred_element_type=j...]
  transfers between devices with their start and end apart: 3 -> 0, of which waited for: 3 -> 0; matrix products, arithmetic and copies ran while one was open for 4% -> 0% of each run, Pallas kernels for 0% -> 0%
where the time goes in v2:
time: 119 us
  Pallas kernels  115 us (97%)
  local copies, waits for them, and re-layouts  2.89 us (2%)
    pallas_call x1, Pallas kernels, body(): pl.pallas_call(kernel, out_shape=(jax.ShapeDtypeStruct((TOK, FB), BF16),...  115 us
    unnamed x4, local copies, waits for them, and re-layouts  2.89 us

profile of v2, /device:TPU:6, one launch (start us, length us, event | category | flops | bytes accessed | tf_op | source)
XLA Modules:
  0.0 119.0 jit_solution(9022644659412479147)
XLA Ops:
  0.6 115.5 %shard_map.59 = (bf16[1024,384]{1,0:T(8,128)(2,1)}, bf16[512,384]{1,0:T(8,128)(2,1)}) custom-call(bf16[1024,384]{1,0:T(8,128)(2,1)} %hid_hbm.1, bf16[16,4096]{1,0:T(8,128)(2,1)} %cot_hbm.1, bf16[512,384]{1,0:T(8,128)(2,1)} %codes_hbm.1, bf16[4,384]{1,0:T(4,128)(2,1)} %scales_ref.1), custom_call_target="tpu_custom_call" | custom-call | flops 6442450944 | bytes 4194304 | tf_op jit(solution)/shard_map/pallas_call | solution.py:327
  116.1 0.0 copy-start
  116.1 2.1 %copy.8 = bf16[1024,384]{1,0:T(8,128)(2,1)} copy(bf16[1024,384]{1,0:T(8,128)(2,1)} %get-tuple-element.4) | data formatting | bytes 1572864
  118.3 0.0 copy-done
  118.3 0.7 copy.9
Async XLA Ops:
  116.1 2.2 %copy-start = (bf16[512,384]{1,0:T(8,128)(2,1)S(1)}, bf16[512,384]{1,0:T(8,128)(2,1)}, u32[]{:S(2)}) copy-start(bf16[512,384]{1,0:T(8,128)(2,1)} %get-tuple-element.5) | copy-start | bytes 1179652

commit v3 on v2

--- a/solution.py
+++ b/solution.py
@@ -12,14 +12,40 @@
 D, FB, TOK, ROWS, QB = 4096, 384, 1024, 16, 128
 OWN = D // 8
 HALF = D // 2
-FZ = 2
+FZ = 4
 CW = 4
 CG = 3
+WH = 1
+GH = 1
+WS, GS = NZ // WH, NZ // GH
 F32, BF16 = jnp.float32, jnp.bfloat16
 
 
 def schedule():
-    return [('own',), ('weights',), ('turn',), ('z', 1, 0), ('z', 1, 1), ('xf', 0), ('z', 2, 0), ('z', 2, 1), ('z', 3, 0), ('z', 3, 1), ('xf', 1), ('near_weights',), ('z', 4, 0), ('xh', 0), ('z', 4, 1), ('w', 0, 0), ('w', 0, 1), ('w', 0, 2), ('w', 0, 3), ('z', 5, 0), ('z', 5, 1), ('xf', 2), ('near_halves',), ('w', 1, 0), ('w', 1, 1), ('z', 6, 0), ('z', 6, 1), ('w', 1, 2), ('xf', 3), ('w', 1, 3), ('z', 7, 0), ('z', 7, 1), ('xh', 1), ('w', 2, 0), ('w', 2, 1), ('w', 2, 2), ('xf', 4), ('w', 2, 3), ('xh', 2), ('xf', 5), ('w', 3, 0), ('w', 3, 1), ('w', 3, 2), ('xf', 6), ('xh', 3), ('w', 3, 3), ('xf', 7), ('xh', 6), ('w', 4, 0), ('xh', 7), ('xh', 4), ('xh', 5), ('w', 4, 1), ('w', 4, 2), ('w', 4, 3), ('w', 5, 0), ('cores',), ('term', 1, 2), ('w', 5, 1), ('gh', 1, 0), ('gh', 1, 1), ('gh', 1, 2), ('term', 1, 1), ('term', 1, -1), ('w', 5, 2), ('w', 5, 3), ('term', 1, 0), ('term', 0, 2), ('gn', 1, 0), ('gh', 0, 0), ('gh', 0, 1), ('gh', 0, 2), ('term', 0, 1), ('w', 6, 0), ('gn', 1, 1), ('term', 0, -1), ('w', 6, 1), ('term', 0, 0), ('gn', 1, 2), ('hid', 0, 0), ('w', 6, 2), ('hid', 0, 1), ('hid', 0, 2), ('w', 6, 3), ('gs', 0), ('hid', 0, 3), ('w', 7, 0), ('gn', 0, 0), ('w', 7, 1), ('gn', 0, 1), ('w', 7, 2), ('w', 7, 3), ('gn', 0, 2), ('g', 1, 0), ('gs', 1), ('far_weights',), ('gs', 2), ('g', 2, 0), ('g', 1, 1), ('ns', 0), ('g', 1, 2), ('g', 3, 0), ('ns', 1), ('g', 2, 1), ('g', 2, 2), ('ns', 2), ('g', 4, 0), ('g', 3, 1), ('g', 3, 2), ('g', 5, 0), ('g', 4, 1), ('g', 4, 2), ('far_forward',), ('g', 6, 0), ('g', 5, 1), ('g', 5, 2), ('g', 7, 0), ('far_halves',), ('hid', 1, 0), ('hid', 1, 1), ('g', 6, 1), ('hid', 1, 2), ('hid', 1, 3), ('g', 6, 2), ('left', 0), ('end', 0), ('g', 7, 1), ('g', 7, 2), ('end', 1), ('end', 2)]
+    return [
+        ("own",), ("weights",), ("w", 0, 0), ("z", 1, 0), ("z", 1, 1), ("z", 1, 2), ("z", 1, 3),
+        ("xf", 0), ("w", 0, 1), ("z", 2, 0), ("z", 2, 1), ("z", 2, 2), ("z", 2, 3), ("z", 3, 0),
+        ("z", 3, 1), ("z", 3, 2), ("z", 3, 3), ("w", 0, 2), ("z", 4, 0), ("z", 4, 1), ("xf", 1),
+        ("near_weights",), ("z", 4, 2), ("z", 4, 3), ("w", 0, 3), ("z", 5, 0), ("z", 5, 1),
+        ("z", 5, 2), ("z", 5, 3), ("xf", 2), ("w", 1, 0), ("z", 6, 0), ("z", 6, 1), ("z", 6, 2),
+        ("z", 6, 3), ("w", 1, 1), ("z", 7, 0), ("w", 1, 2), ("xf", 3), ("z", 7, 1), ("z", 7, 2),
+        ("w", 1, 3), ("z", 7, 3), ("w", 2, 0), ("xh", 1), ("w", 2, 1), ("w", 2, 2), ("xf", 4),
+        ("w", 2, 3), ("xf", 5), ("w", 3, 0), ("turn",), ("xf", 6), ("w", 3, 1), ("xh", 0),
+        ("xf", 7), ("w", 3, 2), ("xh", 2), ("w", 3, 3), ("xh", 3), ("w", 4, 0), ("xh", 5),
+        ("w", 4, 1), ("xh", 4), ("xh", 6), ("w", 4, 2), ("xh", 7), ("w", 4, 3), ("near_halves",),
+        ("cores",), ("w", 5, 0), ("term", 1, 2), ("gh", 1, 0), ("w", 5, 1), ("gh", 1, 2),
+        ("gh", 1, 1), ("w", 5, 2), ("term", 0, 2), ("w", 5, 3), ("term", 1, 1), ("w", 6, 0),
+        ("term", 1, -1), ("gn", 1, 0), ("w", 6, 1), ("term", 0, 1), ("gn", 1, 2), ("w", 6, 2),
+        ("gn", 1, 1), ("w", 6, 3), ("w", 7, 0), ("w", 7, 1), ("hid", 0, 3), ("w", 7, 2),
+        ("term", 1, 0), ("gs", 0), ("gh", 0, 0), ("gh", 0, 1), ("term", 0, -1), ("w", 7, 3),
+        ("gs", 2), ("gs", 1), ("gh", 0, 2), ("hid", 0, 0), ("far_weights",), ("g", 1, 0),
+        ("g", 1, 2), ("g", 1, 1), ("g", 2, 0), ("gn", 0, 2), ("g", 2, 2), ("g", 2, 1),
+        ("term", 0, 0), ("g", 3, 0), ("g", 3, 2), ("g", 3, 1), ("far_forward",), ("hid", 0, 1),
+        ("g", 4, 0), ("g", 4, 2), ("g", 4, 1), ("g", 5, 0), ("ns", 2), ("g", 5, 2), ("far_halves",),
+        ("gn", 0, 1), ("g", 5, 1), ("g", 6, 0), ("g", 6, 2), ("hid", 0, 2), ("gn", 0, 0),
+        ("g", 6, 1), ("ns", 1), ("g", 7, 0), ("hid", 1, 3), ("g", 7, 2), ("hid", 1, 2), ("g", 7, 1),
+        ("ns", 0), ("left", 0), ("end", 0), ("hid", 1, 0), ("end", 2), ("hid", 1, 1), ("end", 1),
+    ]
 
 
 def kernel(
@@ -44,6 +70,8 @@
     ways_x = (at(dx=1), at(dx=-1))
     ways_y = (at(dy=1), at(dy=-1))
     ways_z = (at(dz=1), at(dz=-1))
+    ways_w = (at(dz=WH), at(dz=-WH))
+    ways_g = (at(dz=GH), at(dz=-GH))
     def remote(src, dst, s, r, to):
         return pltpu.make_async_remote_copy(
             src_ref=src, dst_ref=dst, send_sem=s, recv_sem=r, device_id=to, device_id_type=MESH
@@ -173,15 +201,15 @@
             landed(wrelay.at[s - 1, c], wz_r.at[s - 1, c])
         for d in range(2):
             src = weight_piece(node, d, c) if s == 0 else wrelay.at[s - 1, c, d]
-            dst = wrelay.at[s, c, d]
-            if s == NZ - 1:
-                z = zh * NZ + zl + (1 if d == 0 else -1) + 2 * NZ
+            dst = wrelay.at[min(s, WS - 2), c, d]
+            if s == WS - 1:
+                z = zh * NZ + zl + (WH if d == 0 else -WH) + 2 * NZ
                 dst = weight_piece((1 - (z // NZ) % 2) * NY + y, d, c)
-            send(src, dst, wz_s.at[0], wz_r.at[s, c], ways_z[d])
+            send(src, dst, wz_s.at[0], wz_r.at[s, c], ways_w[d])
 
     def go_far_weights():
         for c in range(CW):
-            landed(wrelay.at[0, c], wz_r.at[NZ - 1, c])
+            landed(wrelay.at[0, c], wz_r.at[WS - 1, c])
         weight_y(1)
 
 
@@ -239,16 +267,16 @@
             landed(grelay.at[s, c], gz_r.at[s - 1, c])
         for d in range(2):
             send(
-                grelay.at[s, c, d], grelay.at[s + 1, c, d], gz_s.at[0], gz_r.at[s, c], ways_z[d]
+                grelay.at[s, c, d], grelay.at[s + 1, c, d], gz_s.at[0], gz_r.at[s, c], ways_g[d]
             )
 
     def go_ns(c):
         near_sum[:, units(c), :] = summed(0, c)
 
     def go_end(c):
-        landed(grelay.at[NZ, c], gz_r.at[NZ - 1, c])
-        for d in range(2):
-            total = near_sum[d, units(c), :] + grelay[NZ, c, d].astype(F32)
+        landed(grelay.at[GS, c], gz_r.at[GS - 1, c])
+        for d in range(2):
+            total = near_sum[d, units(c), :] + grelay[GS, c, d].astype(F32)
             wgrad_ref[pl.ds(d * (OWN // 2), OWN // 2), units(c)] = (
                 (total * float(TOK * 8) ** -0.5).T.astype(BF16)
             )
@@ -270,7 +298,7 @@
 
     def go_left(k):
         if k:
-            left(grelay.at[pl.ds(0, NZ)], gz_s.at[0])
+            left(grelay.at[pl.ds(0, GS)], gz_s.at[0])
             return
         left(cot.at[pl.ds(0, 2 * NZ)], x_s.at[0])
         left(cot.at[pl.ds(0, NZ)], xh_s.at[0])
@@ -287,12 +315,14 @@
 
         left(weight.at[pl.ds(0, 4)], wy_s.at[0])
         left(weight.at[pl.ds(0, 2)], wh_s.at[0])
-        left(weight, wz_s.at[0])
+        left(weight.at[pl.ds(0, WS)], wz_s.at[0])
         left(part.at[pl.ds(0, 2)], gh_s.at[0])
         left(part.at[pl.ds(0, 4)], gy_s.at[0])
 
     barrier = pltpu.get_barrier_semaphore()
     peers = [*ways_x, *ways_y, *ways_z, sibling]
+    for hop in sorted({WH, GH} - {1}):
+        peers += (at(dz=hop), at(dz=-hop))
     for peer in peers:
         pl.semaphore_signal(barrier, inc=1, device_id=peer, device_id_type=MESH)
     loads = [
@@ -341,8 +371,8 @@
             pltpu.VMEM((8, 2, FB, OWN // 2), BF16),
             pltpu.VMEM((2, 2, 2, FB, OWN // 2), BF16),
             pltpu.VMEM((2, 2, FB, OWN // 2), BF16),
-            pltpu.VMEM((NZ - 1, CW, 2, OWN // 2 // CW, FB), BF16),
-            pltpu.VMEM((NZ + 1, CG, 2, FB // CG, OWN // 2), BF16),
+            pltpu.VMEM((WS - 1, CW, 2, OWN // 2 // CW, FB), BF16),
+            pltpu.VMEM((GS + 1, CG, 2, FB // CG, OWN // 2), BF16),
             pltpu.VMEM((2, FB, OWN // 2), F32),
             pltpu.VMEM((TOK, FB), F32),
             dma((3,)),
@@ -350,9 +380,9 @@
             dma((1,)), dma((NZ,)), dma((1,)), dma((NZ,)),
             dma((1,)), dma((1,)),
             dma((1,)), dma((2, 2)), dma((1,)), dma((2,)),
-            dma((1,)), dma((NZ, CW)),
+            dma((1,)), dma((WS, CW)),
             dma((1,)), dma((2, CG)), dma((1,)), dma((2, CG)),
-            dma((1,)), dma((NZ, CG)),
+            dma((1,)), dma((GS, CG)),
         ],
         compiler_params=pltpu.CompilerParams(
             collective_id=0, has_side_effects=True, vmem_limit_bytes=56 << 20

time: 119 us -> 110 us (0.924)
  Pallas kernels: 115 us -> 107 us
    pallas_call x1, Pallas kernels: 115 us -> 107 us  [body(): pl.pallas_call(kernel, out_shape=(jax.ShapeDtypeStruct((TOK, FB), BF16),...]
where the time goes in v3:
time: 110 us
  Pallas kernels  107 us (97%)
  local copies, waits for them, and re-layouts  2.89 us (3%)
    pallas_call x1, Pallas kernels, body(): pl.pallas_call(kernel, out_shape=(jax.ShapeDtypeStruct((TOK, FB), BF16),...  107 us
    unnamed x4, local copies, waits for them, and re-layouts  2.89 us

profile of v3, /device:TPU:6, one launch (start us, length us, event | category | flops | bytes accessed | tf_op | source)
XLA Modules:
  0.0 110.1 jit_solution(12322638232794653225)
XLA Ops:
  0.6 106.6 %shard_map.59 = (bf16[1024,384]{1,0:T(8,128)(2,1)}, bf16[512,384]{1,0:T(8,128)(2,1)}) custom-call(bf16[1024,384]{1,0:T(8,128)(2,1)} %hid_hbm.1, bf16[16,4096]{1,0:T(8,128)(2,1)} %cot_hbm.1, bf16[512,384]{1,0:T(8,128)(2,1)} %codes_hbm.1, bf16[4,384]{1,0:T(4,128)(2,1)} %scales_ref.1), custom_call_target="tpu_custom_call" | custom-call | flops 6442450944 | bytes 4194304 | tf_op jit(solution)/shard_map/pallas_call | solution.py:357
  107.2 0.0 copy-start
  107.2 2.1 %copy.8 = bf16[1024,384]{1,0:T(8,128)(2,1)} copy(bf16[1024,384]{1,0:T(8,128)(2,1)} %get-tuple-element.4) | data formatting | bytes 1572864
  109.4 0.0 copy-done
  109.4 0.7 copy.9
Async XLA Ops:
  107.2 2.2 %copy-start = (bf16[512,384]{1,0:T(8,128)(2,1)S(1)}, bf16[512,384]{1,0:T(8,128)(2,1)}, u32[]{:S(2)}) copy-start(bf16[512,384]{1,0:T(8,128)(2,1)} %get-tuple-element.5) | copy-start | bytes 1179652

commit v4 on v3

--- a/solution.py
+++ b/solution.py
@@ -49,9 +49,9 @@
 
 
 def kernel(
-    hid_hbm, cot_hbm, codes_hbm, scales_ref,
+    hid_hbm, cot_hbm, codes_hbm, scales_hbm,
     hgrad_ref, wgrad_ref,
-    cot, hid, hid_t, codes, weight, part, ywhole, yhalf, wrelay, grelay, near_sum, hacc,
+    cot, hid, hid_t, codes, scales, weight, part, ywhole, yhalf, wrelay, grelay, near_sum, hacc,
     local_sem, z_s, z_r, x_s, x_r, xh_s, xh_r, c_s, c_r,
     wy_s, wy_r, wh_s, wh_r, wz_s, wz_r, gy_s, gy_r, gh_s, gh_r, gz_s, gz_r,
 ):
@@ -184,10 +184,11 @@
 
     def go_weights():
         loads[1].wait()
+        loads[3].wait()
         for q in range(OWN // QB):
             rows = pl.ds(q * QB, QB)
             weight[node, rows, :] = (
-                codes[rows, :].astype(F32) * scales_ref[pl.ds(q, 1), :].astype(F32)
+                codes[rows, :].astype(F32) * scales[pl.ds(q, 1), :].astype(F32)
             ).astype(BF16)
         weight_y(0)
 
@@ -329,6 +330,7 @@
         pltpu.make_async_copy(cot_hbm, cot.at[wide], local_sem.at[0]),
         pltpu.make_async_copy(codes_hbm, codes, local_sem.at[1]),
         pltpu.make_async_copy(hid_hbm, hid, local_sem.at[2]),
+        pltpu.make_async_copy(scales_hbm, scales, local_sem.at[3]),
     ]
     for load in loads:
         load.start()
@@ -357,16 +359,17 @@
     return pl.pallas_call(
         kernel,
         out_shape=(
-            jax.ShapeDtypeStruct((TOK, FB), BF16),
-            jax.ShapeDtypeStruct((OWN, FB), BF16),
+            pltpu.VMEM((TOK, FB), BF16),
+            pltpu.VMEM((OWN, FB), BF16),
         ),
-        in_specs=[hbm, hbm, hbm, vmem],
+        in_specs=[hbm, hbm, hbm, hbm],
         out_specs=(vmem, vmem),
         scratch_shapes=[
             pltpu.VMEM((2 * NX * NZ, ROWS, D), BF16),
             pltpu.VMEM((TOK, FB), BF16),
             pltpu.VMEM((FB, TOK), BF16),
             pltpu.VMEM((OWN, FB), BF16),
+            pltpu.VMEM((OWN // QB, FB), BF16),
             pltpu.VMEM((8, OWN, FB), BF16),
             pltpu.VMEM((8, 2, FB, OWN // 2), BF16),
             pltpu.VMEM((2, 2, 2, FB, OWN // 2), BF16),
@@ -375,7 +378,7 @@
             pltpu.VMEM((GS + 1, CG, 2, FB // CG, OWN // 2), BF16),
             pltpu.VMEM((2, FB, OWN // 2), F32),
             pltpu.VMEM((TOK, FB), F32),
-            dma((3,)),
+            dma((4,)),
             dma((2,)), dma((NZ, FZ)),
             dma((1,)), dma((NZ,)), dma((1,)), dma((NZ,)),
             dma((1,)), dma((1,)),

time: 110 us -> 107 us (0.973)
  Pallas kernels: 107 us -> 105 us
  local copies, waits for them, and re-layouts: 2.89 us -> 1.63 us
    pallas_call x1, Pallas kernels: 107 us -> 105 us  [body(): pl.pallas_call(kernel, out_shape=(pltpu.VMEM((TOK, FB), BF16), pltpu.VMEM...]
    unnamed x4 -> x2, local copies, waits for them, and re-layouts: 2.89 us -> 1.63 us
where the time goes in v4:
time: 107 us
  Pallas kernels  105 us (98%)
  local copies, waits for them, and re-layouts  1.63 us (2%)
    pallas_call x1, Pallas kernels, body(): pl.pallas_call(kernel, out_shape=(pltpu.VMEM((TOK, FB), BF16), pltpu.VMEM...  105 us

profile of v4, /device:TPU:6, one launch (start us, length us, event | category | flops | bytes accessed | tf_op | source)
XLA Modules:
  0.0 107.2 jit_solution(9736599571726075362)
XLA Ops:
  0.6 105.0 %shard_map.59 = (bf16[1024,384]{1,0:T(8,128)(2,1)S(1)}, bf16[512,384]{1,0:T(8,128)(2,1)S(1)}) custom-call(bf16[1024,384]{1,0:T(8,128)(2,1)} %hid_hbm.1, bf16[16,4096]{1,0:T(8,128)(2,1)} %cot_hbm.1, bf16[512,384]{1,0:T(8,128)(2,1)} %codes_hbm.1, bf16[4,384]{1,0:T(4,128)(2,1)} %scales_hbm.1), custom_call_target="tpu_custom_call" | custom-call | flops 6442450944 | bytes 4194304 | tf_op jit(solution)/shard_map/pallas_call | solution.py:359
  105.6 0.9 copy.8
  106.5 0.7 copy.9

commit v5 on v4

--- a/solution.py
+++ b/solution.py
@@ -12,7 +12,7 @@
 D, FB, TOK, ROWS, QB = 4096, 384, 1024, 16, 128
 OWN = D // 8
 HALF = D // 2
-FZ = 4
+FZ = 8
 CW = 4
 CG = 3
 WH = 1
@@ -23,28 +23,33 @@
 
 def schedule():
     return [
-        ("own",), ("weights",), ("w", 0, 0), ("z", 1, 0), ("z", 1, 1), ("z", 1, 2), ("z", 1, 3),
-        ("xf", 0), ("w", 0, 1), ("z", 2, 0), ("z", 2, 1), ("z", 2, 2), ("z", 2, 3), ("z", 3, 0),
-        ("z", 3, 1), ("z", 3, 2), ("z", 3, 3), ("w", 0, 2), ("z", 4, 0), ("z", 4, 1), ("xf", 1),
-        ("near_weights",), ("z", 4, 2), ("z", 4, 3), ("w", 0, 3), ("z", 5, 0), ("z", 5, 1),
-        ("z", 5, 2), ("z", 5, 3), ("xf", 2), ("w", 1, 0), ("z", 6, 0), ("z", 6, 1), ("z", 6, 2),
-        ("z", 6, 3), ("w", 1, 1), ("z", 7, 0), ("w", 1, 2), ("xf", 3), ("z", 7, 1), ("z", 7, 2),
-        ("w", 1, 3), ("z", 7, 3), ("w", 2, 0), ("xh", 1), ("w", 2, 1), ("w", 2, 2), ("xf", 4),
-        ("w", 2, 3), ("xf", 5), ("w", 3, 0), ("turn",), ("xf", 6), ("w", 3, 1), ("xh", 0),
-        ("xf", 7), ("w", 3, 2), ("xh", 2), ("w", 3, 3), ("xh", 3), ("w", 4, 0), ("xh", 5),
-        ("w", 4, 1), ("xh", 4), ("xh", 6), ("w", 4, 2), ("xh", 7), ("w", 4, 3), ("near_halves",),
-        ("cores",), ("w", 5, 0), ("term", 1, 2), ("gh", 1, 0), ("w", 5, 1), ("gh", 1, 2),
-        ("gh", 1, 1), ("w", 5, 2), ("term", 0, 2), ("w", 5, 3), ("term", 1, 1), ("w", 6, 0),
-        ("term", 1, -1), ("gn", 1, 0), ("w", 6, 1), ("term", 0, 1), ("gn", 1, 2), ("w", 6, 2),
-        ("gn", 1, 1), ("w", 6, 3), ("w", 7, 0), ("w", 7, 1), ("hid", 0, 3), ("w", 7, 2),
-        ("term", 1, 0), ("gs", 0), ("gh", 0, 0), ("gh", 0, 1), ("term", 0, -1), ("w", 7, 3),
-        ("gs", 2), ("gs", 1), ("gh", 0, 2), ("hid", 0, 0), ("far_weights",), ("g", 1, 0),
-        ("g", 1, 2), ("g", 1, 1), ("g", 2, 0), ("gn", 0, 2), ("g", 2, 2), ("g", 2, 1),
-        ("term", 0, 0), ("g", 3, 0), ("g", 3, 2), ("g", 3, 1), ("far_forward",), ("hid", 0, 1),
-        ("g", 4, 0), ("g", 4, 2), ("g", 4, 1), ("g", 5, 0), ("ns", 2), ("g", 5, 2), ("far_halves",),
-        ("gn", 0, 1), ("g", 5, 1), ("g", 6, 0), ("g", 6, 2), ("hid", 0, 2), ("gn", 0, 0),
-        ("g", 6, 1), ("ns", 1), ("g", 7, 0), ("hid", 1, 3), ("g", 7, 2), ("hid", 1, 2), ("g", 7, 1),
-        ("ns", 0), ("left", 0), ("end", 0), ("hid", 1, 0), ("end", 2), ("hid", 1, 1), ("end", 1),
+        ("own",), ("weights",), ("z", 1, 0), ("z", 1, 1), ("z", 1, 2), ("z", 1, 3), ("z", 1, 4),
+        ("z", 1, 5), ("z", 1, 6), ("z", 1, 7), ("w", 0, 0), ("z", 2, 0), ("z", 2, 1), ("z", 2, 2),
+        ("z", 2, 3), ("z", 2, 4), ("z", 2, 5), ("z", 2, 6), ("z", 2, 7), ("xf", 0), ("z", 3, 0),
+        ("z", 3, 1), ("z", 3, 2), ("w", 0, 1), ("z", 3, 3), ("z", 3, 4), ("z", 3, 5), ("z", 3, 6),
+        ("z", 3, 7), ("z", 4, 0), ("z", 4, 1), ("z", 4, 2), ("z", 4, 3), ("z", 4, 4), ("z", 4, 5),
+        ("z", 4, 6), ("z", 4, 7), ("w", 0, 2), ("z", 5, 0), ("xf", 1), ("z", 5, 1),
+        ("near_weights",), ("z", 5, 2), ("z", 5, 3), ("z", 5, 4), ("z", 5, 5), ("w", 0, 3),
+        ("z", 5, 6), ("z", 5, 7), ("z", 6, 0), ("z", 6, 1), ("w", 1, 0), ("z", 6, 2), ("turn",),
+        ("z", 6, 3), ("z", 6, 4), ("xf", 2), ("z", 6, 5), ("xh", 0), ("z", 6, 6), ("w", 1, 1),
+        ("z", 6, 7), ("z", 7, 0), ("z", 7, 1), ("w", 1, 2), ("z", 7, 2), ("near_halves",),
+        ("xf", 3), ("w", 1, 3), ("z", 7, 3), ("z", 7, 4), ("w", 2, 0), ("z", 7, 5), ("z", 7, 6),
+        ("xf", 4), ("w", 2, 1), ("z", 7, 7), ("w", 2, 2), ("w", 2, 3), ("w", 3, 0), ("xf", 5),
+        ("w", 3, 1), ("xf", 6), ("w", 3, 2), ("w", 3, 3), ("xf", 7), ("xh", 1), ("w", 4, 0),
+        ("xh", 3), ("w", 4, 1), ("w", 4, 2), ("xh", 2), ("xh", 6), ("xh", 4), ("xh", 5), ("xh", 7),
+        ("w", 4, 3), ("w", 5, 0), ("w", 5, 1), ("cores",), ("term", 1, 2), ("gh", 1, 0),
+        ("w", 5, 2), ("term", 1, 1), ("gh", 1, 2), ("w", 5, 3), ("w", 6, 0), ("gh", 1, 1),
+        ("term", 1, -1), ("w", 6, 1), ("gn", 1, 0), ("w", 6, 2), ("term", 0, 1), ("w", 6, 3),
+        ("term", 1, 0), ("w", 7, 0), ("gn", 1, 1), ("w", 7, 1), ("w", 7, 2), ("gn", 1, 2),
+        ("term", 0, 2), ("gs", 0), ("w", 7, 3), ("hid", 0, 1), ("hid", 0, 0), ("gs", 1),
+        ("term", 0, 0), ("g", 1, 0), ("gs", 2), ("g", 1, 1), ("far_weights",), ("g", 2, 0),
+        ("hid", 0, 3), ("g", 1, 2), ("g", 2, 1), ("hid", 0, 2), ("gh", 0, 0), ("gh", 0, 1),
+        ("g", 3, 0), ("g", 2, 2), ("term", 0, -1), ("g", 3, 1), ("g", 4, 0), ("g", 3, 2),
+        ("gh", 0, 2), ("far_forward",), ("g", 4, 1), ("gn", 0, 1), ("g", 4, 2), ("gn", 0, 2),
+        ("g", 5, 1), ("g", 5, 0), ("gn", 0, 0), ("g", 5, 2), ("g", 6, 1), ("far_halves",),
+        ("g", 6, 0), ("hid", 1, 1), ("g", 6, 2), ("hid", 1, 2), ("ns", 1), ("g", 7, 1), ("g", 7, 0),
+        ("ns", 2), ("g", 7, 2), ("hid", 1, 0), ("ns", 0), ("hid", 1, 3), ("left", 0), ("end", 0),
+        ("end", 1), ("end", 2),
     ]
 
 

time: 107 us -> 109 us (1.019); the launches traced: 107 us -> 108 us
  no operation moved by 1% of the time
where the time goes in v5:
time: 109 us; the launch traced here: 108 us
  Pallas kernels  106 us (97%)
  local copies, waits for them, and re-layouts  1.63 us (1%)
    pallas_call x1, Pallas kernels, body(): pl.pallas_call(kernel, out_shape=(pltpu.VMEM((TOK, FB), BF16), pltpu.VMEM...  106 us

profile of v5, /device:TPU:6, one launch (start us, length us, event | category | flops | bytes accessed | tf_op | source)
XLA Modules:
  0.0 108.0 jit_solution(13545711814671655256)
XLA Ops:
  0.6 105.8 %shard_map.59 = (bf16[1024,384]{1,0:T(8,128)(2,1)S(1)}, bf16[512,384]{1,0:T(8,128)(2,1)S(1)}) custom-call(bf16[1024,384]{1,0:T(8,128)(2,1)} %hid_hbm.1, bf16[16,4096]{1,0:T(8,128)(2,1)} %cot_hbm.1, bf16[512,384]{1,0:T(8,128)(2,1)} %codes_hbm.1, bf16[4,384]{1,0:T(4,128)(2,1)} %scales_hbm.1), custom_call_target="tpu_custom_call" | custom-call | flops 6442450944 | bytes 4194304 | tf_op jit(solution)/shard_map/pallas_call | solution.py:364
  106.4 0.9 copy.8
  107.3 0.7 copy.9
